TPU v7x, 256 devices: a whole 4x4x8 slice. The times are simulated.
256 devices in a mesh: island: 8 (over y_lo, x), fsdp: 32 (over z, y_hi, core).
Axes of the slice: x: 4, y: 4 (y_hi: 2, y_lo: 2; y = y_hi * 2 + y_lo), z: 8, core: 2. Of those that a mesh axis runs over, the one named last changes fastest.
Arguments:
- tokens: bfloat16 [65536, 4096], P(('island', 'fsdp')), may hold values from -6 to 6
- target: bfloat16 [65536, 1024], P(('island', 'fsdp')), may hold values from -6 to 6
- kv_weight: bfloat16 [8, 4096, 1024], P('island', 'fsdp'), may hold values from -0.09375 to 0.09375
- norm_gain: float32 [8, 4096], P('island'), may hold values from 0.5 to 1.5
- global_frag: float32 [2, 4096, 1024], P(None, 'fsdp'), may hold values from -6 to 6
- momentum: float32 [2, 4096, 1024], P(None, 'fsdp'), may hold values from -3 to 3
- local_frag: float32 [8, 2, 4096, 1024], P('island', None, 'fsdp'), may hold values from -6 to 6
Outputs:
- weight_grad: bfloat16 [8, 4096, 1024], P('island', 'fsdp')
- token_grad: bfloat16 [65536, 4096], P(('island', 'fsdp'))
- gain_grad: float32 [8, 4096], P('island')
- new_global: float32 [2, 4096, 1024], P(None, 'fsdp')
- new_momentum: float32 [2, 4096, 1024], P(None, 'fsdp')
All inputs are finite; a program needn't handle non-finite values.
Results may differ from a plain program's by a relative error of at most 0.0055.
Values may be sent and summed in bfloat16 or wider, within the bound.
A program may use at most 128 MiB of HBM per device.

v0:
```python
import math

import jax
import jax.numpy as jnp
from jax import lax
from jax.sharding import PartitionSpec as P


def on_device(tokens, target, kv_weight, norm_gain, global_frag, momentum, local_frag):
    weight_shard = kv_weight[0]
    gain_row = norm_gain[0]
    tokens_f = tokens.astype(jnp.float32)
    inverse = lax.rsqrt(jnp.mean(tokens_f * tokens_f, axis=1, keepdims=True) + 1e-05)
    scaled = tokens_f * inverse
    normed = (scaled * gain_row[None, :]).astype(jnp.bfloat16)
    token_count = tokens.shape[0] * lax.axis_size("fsdp")
    loss_scale = 1.0 / math.sqrt(token_count)
    target_f = target.astype(jnp.float32)
    full_weight = lax.all_gather(weight_shard, "fsdp", axis=0, tiled=True)
    projected = jnp.dot(normed, full_weight, preferred_element_type=jnp.float32)
    error = (projected - target_f).astype(jnp.bfloat16)
    back = lax.dot_general(
        error, full_weight, (((1,), (1,)), ((), ())), preferred_element_type=jnp.float32
    )
    product = lax.dot_general(
        normed, error, (((0,), (0,)), ((), ())), preferred_element_type=jnp.float32
    )
    weight_grad = lax.psum_scatter(
        loss_scale * product, "fsdp", scatter_dimension=0, tiled=True
    ).astype(jnp.bfloat16)
    gain_grad = lax.psum(jnp.sum(back * scaled, axis=0), "fsdp")
    weighted = back * gain_row[None, :]
    token_grad = inverse * (weighted - scaled * jnp.mean(weighted * scaled, axis=1, keepdims=True))
    token_grad = token_grad.astype(jnp.bfloat16)
    drift = global_frag - local_frag[0]
    islands = lax.axis_size("island")
    outer_grad = lax.psum(drift, "island") / islands
    new_momentum = 0.9 * momentum + outer_grad
    new_global = global_frag - 0.7 * (outer_grad + 0.9 * new_momentum)
    return (weight_grad[None], token_grad, gain_grad[None], new_global, new_momentum)


def solution(mesh):
    placed = (
        P(("island", "fsdp"), None),
        P(("island", "fsdp"), None),
        P("island", "fsdp", None),
        P("island", None),
        P(None, "fsdp", None),
        P(None, "fsdp", None),
        P("island", None, "fsdp", None),
    )
    return jax.shard_map(
        on_device,
        mesh=mesh,
        in_specs=placed,
        out_specs=(
            P("island", "fsdp", None),
            P(("island", "fsdp"), None),
            P("island", None),
            P(None, "fsdp", None),
            P(None, "fsdp", None),
        ),
        check_vma=False,
    )
```

profile of v0, /device:TPU:2, one launch (start us, length us, event | category | flops | bytes accessed | tf_op | source)
XLA Modules:
  0.0 369.0 jit_solution(14870135365026844564)
XLA Ops:
  8.0 0.0 copy-start
  8.0 0.0 copy-start.4
  8.0 0.0 copy-start.5
  8.0 0.0 all-gather.3.cloned.1.call-start
  8.1 0.7 all-gather.3.cloned.1.call-update
  8.8 0.0 all-reduce.2.cloned.1.call-start
  8.8 2.7 bitcast_subtract_fusion
  11.5 0.0 all-reduce.2.cloned.1.call-update
  11.5 0.0 reduce-scatter.2.cloned.1.call-start
  11.6 0.0 copy-done
  11.6 0.5 fusion.14
  12.1 104.5 %all-gather.3.cloned.1.call-done = bf16[1,4096,1024]{2,1,0:T(8,128)(2,1)} async-done(((bf16[1,128,1024]{2,1,0:T(8,128)(2,1)}), bf16[1,4096,1024]{2,1,0:T(8,128)(2,1)}) %all-gather.3.cloned.1.call-update) | async-done | bytes 8388624 | tf_op jit(solution)/shard_map/all_gather | solution.py:19
  116.6 0.0 copy-done.4
  116.6 0.0 copy-done.5
  116.6 5.8 %fusion.18 = bf16[256,1024]{1,0:T(8,128)(2,1)S(1)} fusion(bf16[1,4096,1024]{2,1,0:T(8,128)(2,1)} %all-gather.3.cloned.1.call-done, bf16[256,1024]{1,0:T(8,128)(2,1)S(1)} %copy-done.5, bf16[256,4096]{1,0:T(8,128)(2,1)S(1)} %copy-done, f32[4096]{0:T(1024)S(1)} %bitcast.19, f32[256]{0:T(256)S(1)} %add_rsqrt_fusion), kind=kOutput, calls=%fused_computation.19 | convolution fusion | flops 2152464384 | bytes 11551744 | tf_op jit(solution)/shard_map/dot_general | solution.py:20
  122.4 0.0 copy-start.2
  122.4 0.8 copy-done.2
  123.2 8.4 %convolution_multiply_fusion = f32[4096,1024]{1,0:T(8,128)} fusion(bf16[256,1024]{1,0:T(8,128)(2,1)S(1)} %fusion.18, bf16[256,4096]{1,0:T(8,128)(2,1)S(1)} %copy-done, f32[4096]{0:T(1024)S(1)} %bitcast.20, f32[256]{0:T(256)S(1)} %add_rsqrt_fusion), kind=kOutput, calls=%fused_computation | convolution fusion | flops 2155872256 | bytes 19416064 | tf_op jit(solution)/shard_map/dot_general | solution.py:25
  131.5 0.0 copy-start.1
  131.5 0.0 reduce-scatter.2.cloned.1.call-update
  131.5 0.0 all-reduce.2.cloned.1.call-done
  131.6 1.2 copy-done.1
  132.7 0.0 copy-start.3
  132.7 3.4 multiply_subtract_fusion
  136.1 0.0 copy-done.3
  136.1 8.2 %fusion.13 = (f32[4096]{0:T(1024)S(1)}, f32[256]{0:T(256)S(1)}, f32[256,4096]{1,0:T(8,128)}) fusion(bf16[256,4096]{1,0:T(8,128)(2,1)S(1)} %copy-done, f32[256]{0:T(256)S(1)} %add_rsqrt_fusion, f32[4096]{0:T(1024)S(1)} %bitcast.21, bf16[256,1024]{1,0:T(8,128)(2,1)S(1)} %copy-done.3, bf16[1,4096,1024]{2,1,0:T(8,128)(2,1)} %all-gather.3.cloned.1.call-done), kind=kOutput, calls=%fused_computation.16 | convolution fusion | flops 2154819328 | bytes 15239168 | tf_op jit(solution)/shard_map/dot_general | solution.py:22
  144.3 132.2 %psum.14 = f32[1,4096]{1,0:T(1,128)} all-reduce(f32[1,4096]{1,0:T(1,128)S(1)} %bitcast.23), channel_id=1, replica_groups=mesh['island'=8,'fsdp'=32] {'fsdp'}, use_global_device_ids=true, to_apply=%region_4.0 | all-reduce | flops 4096 | bytes 32768 | tf_op jit(solution)/shard_map/psum | solution.py:31
  276.5 4.7 %fusion.12 = bf16[256,4096]{1,0:T(8,128)(2,1)} fusion(bf16[256,4096]{1,0:T(8,128)(2,1)S(1)} %copy-done, f32[256,4096]{1,0:T(8,128)} %get-tuple-element.9, f32[256]{0:T(256)S(1)} %broadcast_multiply_fusion, f32[4096]{0:T(1024)S(1)} %bitcast.22, f32[256]{0:T(256)S(1)} %add_rsqrt_fusion), kind=kLoop, calls=%fused_computation.15 | loop fusion | flops 7340032 | bytes 8407040 | tf_op jit(solution)/shard_map/convert_element_type | solution.py:34
  281.1 78.7 %reduce-scatter.2.cloned.1.call-done = f32[128,1024]{1,0:T(8,128)} async-done(((f32[4096,1024]{1,0:T(8,128)}), f32[128,1024]{1,0:T(8,128)}) %reduce-scatter.2.cloned.1.call-update) | async-done | bytes 524304 | tf_op jit(solution)/shard_map/reduce_scatter | solution.py:28
  359.8 1.8 convert_bitcast_fusion
  (2 shorter events, 0.0 us)
Async XLA Ops:
  8.0 3.6 copy-start
  8.0 108.6 %copy-start.4 = (f32[1,4096]{1,0:T(1,128)S(1)}, f32[1,4096]{1,0:T(1,128)}, u32[]{:S(2)}) copy-start(f32[1,4096]{1,0:T(1,128)} %param.10) | copy-start | bytes 49156
  8.0 108.6 %copy-start.5 = (bf16[256,1024]{1,0:T(8,128)(2,1)S(1)}, bf16[256,1024]{1,0:T(8,128)(2,1)}, u32[]{:S(2)}) copy-start(bf16[256,1024]{1,0:T(8,128)(2,1)} %param.8) | copy-start | bytes 1572868
  8.0 108.6 %all-gather.3.cloned.1.call-start = ((), (), s32[]{:S(2)}) async-start(), calls=%async_computation.3 | async-start | bytes 8650752 | tf_op jit(solution)/shard_map/all_gather | solution.py:19
  8.8 122.8 %all-reduce.2.cloned.1.call-start = ((), (), s32[]{:S(2)}) async-start(), calls=%async_computation.2 | async-start | bytes 2097152 | tf_op jit(solution)/shard_map/psum | solution.py:37
  11.5 348.3 %reduce-scatter.2.cloned.1.call-start = ((), (), s32[]{:S(2)}) async-start(), calls=%async_computation.1 | async-start | bytes 17301504 | tf_op jit(solution)/shard_map/reduce_scatter | solution.py:28
  122.4 0.8 copy-start.2
  131.5 1.2 copy-start.1
  132.7 3.4 copy-start.3
Sparse Core Ops, SparseCore 0:
  11.7 104.8 all-gather.2
  131.7 228.1 reduce-scatter.1
Sparse Core Ops, SparseCore 1:
  12.6 83.5 all-reduce.1
where the time goes:
time: 369 us
  waiting for transfers between devices  184 us (50%)
  blocking collectives  132 us (36%)
  matrix products  22.3 us (6%)
  between operations  15.5 us (4%)
  other arithmetic  13 us (4%)
    psum x1, blocking collectives, on_device(): gain_grad = lax.psum(jnp.sum(back * scaled, axis=0), 'fsdp')  132 us
    all_gather x1, waiting for transfers between devices, on_device(): full_weight = lax.all_gather(weight_shard, 'fsdp', axis=0, tiled=True)  104 us
    reduce_scatter x1, waiting for transfers between devices, on_device(): lax.psum_scatter(loss_scale * product, 'fsdp', scatter_dimension=0, tiled...  78.7 us
    dot_general x1, matrix products, on_device(): lax.dot_general(normed, error, (((0,), (0,)), ((), ())), preferred_elemen...  8.35 us
    dot_general x1, matrix products, on_device(): lax.dot_general(error, full_weight, (((1,), (1,)), ((), ())), preferred_e...  8.22 us
  transfers between devices with their start and end apart: 3, of which 2 were waited for; matrix products, arithmetic and copies ran while one was open for 9% of the time, Pallas kernels for 0%

commit v1 on v0

v1 whole, which is shorter than its diff:
```python
import math

import jax
import jax.numpy as jnp
from jax import lax
from jax.experimental import pallas as pl
from jax.experimental.pallas import tpu as pltpu
from jax.sharding import PartitionSpec as P

MESH = pl.DeviceIdType.MESH
BF16 = jnp.bfloat16
F32 = jnp.float32
NQ = 4
QC = 256
NZ = 8
TOK = 256
D = 4096
PLUS, MINUS = 0, 1
NSEND = 160


def hops(q, way):
    return 4 if (q % 2) == way else 3


def nt_dot(a, b):
    return lax.dot_general(a, b, (((1,), (1,)), ((), ())), preferred_element_type=F32)


def kernel(
    tok_h, tgt_h, w_h, gain_h, glob_h, mom_h, loc_h,
    wg_h, tg_h, gg_h, ng_h, nm_h,
    tok, tgt, gain, glob, mom, loc, wb, normed, nto, ntr, errb, rss, rsr, back, tgo, wgo,
    ds, dr, osb, go, gc, g1, gy, g2, gz, gsum, rowacc, inv_ref,
    ld, st, send, ag_sem, y_sem, sib_sem, nt_sem, err_sem, rs_sem, d_sem, o_sem, g_sem, gz_sem,
):
    isl = lax.axis_index("island")
    fs = lax.axis_index("fsdp")
    z = fs // 4
    yh = (fs // 2) % 2
    c = fs % 2

    def at(zz, yy, cc):
        return (isl, (zz * 2 + yy) * 2 + cc)

    def mod8(v):
        return lax.rem(v + 8, 8)

    ring = (at(mod8(z + 1), yh, c), at(mod8(z - 1), yh, c))
    sib = at(z, yh, 1 - c)
    flip = at(z, 1 - yh, c)
    diag = at(z, 1 - yh, 1 - c)

    sends = []

    def push(src, dst, sem, dev):
        cp = pltpu.make_async_remote_copy(
            src_ref=src, dst_ref=dst, send_sem=send.at[len(sends)], recv_sem=sem,
            device_id=dev, device_id_type=MESH)
        cp.start()
        sends.append(cp)

    def arrived(ref, sem):
        pltpu.make_async_copy(ref, ref, sem).wait()

    loads_w = [pltpu.make_async_copy(
        w_h.at[:, pl.ds(q * QC, QC)], wb.at[q, c, z, pl.ds(yh * 128, 128)], ld.at[q]) for q in range(NQ)]
    for cp in loads_w:
        cp.start()
    loads = [pltpu.make_async_copy(s, d, ld.at[NQ + i]) for i, (s, d) in enumerate(
        ((tok_h, tok), (gain_h, gain), (tgt_h, tgt), (glob_h, glob), (loc_h, loc), (mom_h, mom)))]
    for cp in loads:
        cp.start()

    bar = pltpu.get_barrier_semaphore()
    partners = [at(mod8(z + o), yh, c) for o in range(1, NZ)] + [sib, flip, diag]
    partners += [(lax.rem(isl + o, 8), fs) for o in range(1, 8)]
    for dev in partners:
        pl.semaphore_signal(bar, inc=1, device_id=dev, device_id_type=MESH)
    pl.semaphore_wait(bar, len(partners))

    def own_half(q, yy):
        return wb.at[q, c, z, pl.ds(yy * 128, 128)]

    def ring_own(q, yy):
        for way in (PLUS, MINUS):
            push(own_half(q, yy), own_half(q, yy), ag_sem.at[q, way, 0], ring[way])

    for q in range(NQ):
        loads_w[q].wait()
        push(own_half(q, yh), own_half(q, yh), y_sem.at[q], flip)
        if q < 2:
            ring_own(q, yh)

    def to_sib(q, zz):
        push(wb.at[q, c, zz], wb.at[q, c, zz], sib_sem.at[q], sib)

    def ring_other(q):
        arrived(own_half(q, 1 - yh), y_sem.at[q])
        ring_own(q, 1 - yh)

    loads[0].wait()

    def squares(i, acc):
        t = tok[:, pl.ds(pl.multiple_of(i * 128, 128), 128)].astype(F32)
        return acc + t * t

    acc = lax.fori_loop(0, 32, squares, jnp.zeros((TOK, 128), F32), unroll=4)
    inv_ref[...] = jnp.broadcast_to(
        lax.rsqrt(jnp.sum(acc, axis=1, keepdims=True) / D + 1e-05), (TOK, 128))

    for q in (0, 1):
        ring_other(q)
    for q in (0, 1):
        to_sib(q, z)

    loads[1].wait()

    def norm_block(i, _):
        bc, bz, by = i // 16, (i // 2) % 8, i % 2
        f = (bz * 2 + by) * 2 + bc
        cols = pl.ds(pl.multiple_of(f * 128, 128), 128)
        n = (tok[:, cols].astype(F32) * inv_ref[...] * gain[:, cols]).astype(BF16)
        normed[:, pl.ds(pl.multiple_of(i * 128, 128), 128)] = n
        nto[by, bc, bz] = n.T
        return 0

    lax.fori_loop(0, 32, norm_block, 0, unroll=2)
    push(nto.at[yh, 1 - c], ntr.at[0], nt_sem.at[0], sib)
    push(nto.at[1 - yh, c], ntr.at[1], nt_sem.at[1], flip)
    push(nto.at[1 - yh, 1 - c], ntr.at[2], nt_sem.at[2], diag)

    def gather_step(half, s):
        for q in (2 * half, 2 * half + 1):
            for way in (PLUS, MINUS):
                k = hops(q, way)
                if s > k:
                    continue
                zz = mod8(z - s) if way == PLUS else mod8(z + s)
                arrived(wb.at[q, c, zz], ag_sem.at[q, way, s - 1])
                if s < k:
                    push(wb.at[q, c, zz], wb.at[q, c, zz], ag_sem.at[q, way, s], ring[way])
                to_sib(q, zz)

    def project(half):
        for q in (2 * half, 2 * half + 1):
            arrived(wb.at[q, 1 - c], sib_sem.at[q])
            p = jnp.dot(normed[...], wb[q].reshape(D, QC), preferred_element_type=F32)
            errb[0, q] = (p - tgt[:, q * QC:(q + 1) * QC].astype(F32)).astype(BF16)
            push(errb.at[0, q], errb.at[2, q], err_sem.at[1, q], flip)
            push(errb.at[0, q], errb.at[1, q], err_sem.at[0, q], sib)

    def pass_error(half):
        for q in (2 * half, 2 * half + 1):
            arrived(errb.at[2, q], err_sem.at[1, q])
            push(errb.at[2, q], errb.at[3, q], err_sem.at[2, q], sib)

    def have_error(half):
        for q in (2 * half, 2 * half + 1):
            arrived(errb.at[1, q], err_sem.at[0, q])
            arrived(errb.at[3, q], err_sem.at[2, q])

    def term(q, zz):
        p = jnp.dot(nto[yh, c, zz], errb[0, q], preferred_element_type=F32)
        for r in range(3):
            p += jnp.dot(ntr[r, zz], errb[r + 1, q], preferred_element_type=F32)
        return p

    def reduce_step(half, s):
        for q in (2 * half, 2 * half + 1):
            for way in (PLUS, MINUS):
                k = hops(q, way)
                if s >= k:
                    continue
                p = term(q, mod8(z + (k - s)) if way == PLUS else mod8(z - (k - s)))
                if s > 0:
                    arrived(rsr.at[q, way, s - 1], rs_sem.at[q, way, s - 1])
                    p += rsr[q, way, s - 1].astype(F32)
                rss[q, way, s] = p.astype(BF16)
                push(rss.at[q, way, s], rsr.at[q, way, s], rs_sem.at[q, way, s], ring[way])

    loss_scale = 1.0 / math.sqrt(TOK * 32)

    def reduce_last(half):
        for q in (2 * half, 2 * half + 1):
            p = term(q, z)
            for way in (PLUS, MINUS):
                s = hops(q, way) - 1
                arrived(rsr.at[q, way, s], rs_sem.at[q, way, s])
                p += rsr[q, way, s].astype(F32)
            wgo[:, q * QC:(q + 1) * QC] = (p * loss_scale).astype(BF16)

    def drift_out():
        loads[3].wait()
        loads[4].wait()

        def one(j, _):
            rows = pl.ds(pl.multiple_of(j * 32, 32), 32)
            ds[j] = (glob[rows, :] - loc[rows, :]).astype(BF16)
            return 0

        lax.fori_loop(0, 8, one, 0)
        for o in range(1, 8):
            j = lax.rem(isl + o, 8)
            push(ds.at[j], dr.at[isl], d_sem.at[isl], (j, fs))
        dr[isl] = ds[isl]

    def drift_sum():
        for o in range(1, 8):
            j = lax.rem(isl + o, 8)
            arrived(dr.at[j], d_sem.at[j])
        total = dr[0].astype(F32)
        for j in range(1, 8):
            total += dr[j].astype(F32)
        osb[isl] = (total / 8).astype(BF16)
        for o in range(1, 8):
            j = lax.rem(isl + o, 8)
            push(osb.at[isl], osb.at[isl], o_sem.at[isl], (j, fs))

    def outer_step():
        loads[5].wait()
        for o in range(1, 8):
            j = lax.rem(isl + o, 8)
            arrived(osb.at[j], o_sem.at[j])

        def one(j, _):
            rows = pl.ds(pl.multiple_of(j * 32, 32), 32)
            outer = osb[j].astype(F32)
            nm = 0.9 * mom[rows, :] + outer
            mom[rows, :] = nm
            glob[rows, :] = glob[rows, :] - 0.7 * (outer + 0.9 * nm)
            return 0

        lax.fori_loop(0, 8, one, 0)
        stores.append(pltpu.make_async_copy(mom, nm_h, st.at[0]))
        stores[-1].start()
        stores.append(pltpu.make_async_copy(glob, ng_h, st.at[1]))
        stores[-1].start()

    stores = []

    def back_blocks(lo, hi):
        def one(kb, _):
            bc, bz = kb // 8, kb % 8
            b = nt_dot(errb[0, 0], wb[0, bc, bz])
            for q in range(1, NQ):
                b += nt_dot(errb[0, q], wb[q, bc, bz])
            for by in range(2):
                f = (bz * 2 + by) * 2 + bc
                cols = pl.ds(pl.multiple_of(f * 128, 128), 128)
                bb = b[:, by * 128:(by + 1) * 128]
                sc = tok[:, cols].astype(F32) * inv_ref[...]
                bs = bb * sc
                go[pl.ds(f, 1), :] = jnp.sum(bs, axis=0, keepdims=True)
                rowacc[...] += bs * gain[:, cols]
                back[:, cols] = bb
            return 0

        lax.fori_loop(lo, hi, one, 0)

    def token_grad():
        m = jnp.sum(rowacc[...], axis=1, keepdims=True) / D

        def one(f, _):
            cols = pl.ds(pl.multiple_of(f * 128, 128), 128)
            iv = inv_ref[...]
            sc = tok[:, cols].astype(F32) * iv
            tgo[:, cols] = (iv * (back[:, cols] * gain[:, cols] - sc * m)).astype(BF16)
            return 0

        lax.fori_loop(0, 32, one, 0)
        stores.append(pltpu.make_async_copy(tgo, tg_h, st.at[2]))
        stores[-1].start()

    gather_step(0, 1)
    drift_out()
    gather_step(0, 2)
    for q in (2, 3):
        ring_own(q, yh)
        ring_other(q)
    for q in (2, 3):
        to_sib(q, z)
    gather_step(0, 3)
    loads[2].wait()
    gather_step(0, 4)
    project(0)
    gather_step(1, 1)
    pass_error(0)
    drift_sum()
    gather_step(1, 2)
    have_error(0)
    for r in range(3):
        arrived(ntr.at[r], nt_sem.at[r])
    gather_step(1, 3)
    outer_step()
    gather_step(1, 4)
    reduce_step(0, 0)
    project(1)
    reduce_step(0, 1)
    pass_error(1)
    rowacc[...] = jnp.zeros_like(rowacc)
    reduce_step(0, 2)
    have_error(1)
    reduce_step(1, 0)
    back_blocks(0, 8)
    reduce_step(0, 3)
    reduce_step(1, 1)
    back_blocks(8, 16)
    push(go, gc, g_sem.at[0], sib)
    reduce_step(1, 2)
    arrived(gc, g_sem.at[0])
    g1[...] = go[...] + gc[...]
    push(g1, gy, g_sem.at[1], flip)
    reduce_last(0)
    reduce_step(1, 3)
    arrived(gy, g_sem.at[1])
    g2[...] = g1[...] + gy[...]
    for o in range(1, NZ):
        push(g2, gz.at[z], gz_sem.at[z], at(mod8(z + o), yh, c))
    gz[z] = g2[...]
    token_grad()
    reduce_last(1)
    stores.append(pltpu.make_async_copy(wgo, wg_h, st.at[3]))
    stores[-1].start()
    for o in range(1, NZ):
        zz = mod8(z + o)
        arrived(gz.at[zz], gz_sem.at[zz])
    total = gz[0]
    for j in range(1, NZ):
        total += gz[j]
    gsum[...] = total
    stores.append(pltpu.make_async_copy(gsum, gg_h, st.at[4]))
    stores[-1].start()
    for cp in sends:
        cp.wait_send()
    for cp in stores:
        cp.wait()


def on_device(tokens, target, kv_weight, norm_gain, global_frag, momentum, local_frag):
    sem = pltpu.SemaphoreType.DMA
    vm = pltpu.VMEM
    anyspec = pl.BlockSpec(memory_space=pl.ANY)
    outs = (
        jax.ShapeDtypeStruct((128, 1024), BF16),
        jax.ShapeDtypeStruct((TOK, D), BF16),
        jax.ShapeDtypeStruct((32, 128), F32),
        jax.ShapeDtypeStruct((256, 1024), F32),
        jax.ShapeDtypeStruct((256, 1024), F32),
    )
    wg, tg, gg, ng, nm = pl.pallas_call(
        kernel,
        out_shape=outs,
        in_specs=[anyspec] * 7,
        out_specs=[anyspec] * 5,
        scratch_shapes=[
            vm((TOK, D), BF16),
            vm((TOK, 1024), BF16),
            vm((1, D), F32),
            vm((256, 1024), F32),
            vm((256, 1024), F32),
            vm((256, 1024), F32),
            vm((NQ, 2, NZ, 256, QC), BF16),
            vm((TOK, D), BF16),
            vm((2, 2, NZ, 128, TOK), BF16),
            vm((3, NZ, 128, TOK), BF16),
            vm((4, NQ, TOK, QC), BF16),
            vm((NQ, 2, 4, 128, QC), BF16),
            vm((NQ, 2, 4, 128, QC), BF16),
            vm((TOK, D), F32),
            vm((TOK, D), BF16),
            vm((128, 1024), BF16),
            vm((8, 32, 1024), BF16),
            vm((8, 32, 1024), BF16),
            vm((8, 32, 1024), BF16),
            vm((32, 128), F32),
            vm((32, 128), F32),
            vm((32, 128), F32),
            vm((32, 128), F32),
            vm((32, 128), F32),
            vm((NZ, 32, 128), F32),
            vm((32, 128), F32),
            vm((TOK, 128), F32),
            vm((TOK, 128), F32),
            sem((NQ + 6,)),
            sem((5,)),
            sem((NSEND,)),
            sem((NQ, 2, 4)),
            sem((NQ,)),
            sem((NQ,)),
            sem((3,)),
            sem((3, NQ)),
            sem((NQ, 2, 4)),
            sem((8,)),
            sem((8,)),
            sem((2,)),
            sem((NZ,)),
        ],
        compiler_params=pltpu.CompilerParams(
            collective_id=0, has_side_effects=True, vmem_limit_bytes=60 * 2**20),
        cost_estimate=pl.CostEstimate(flops=6 * 2**30, bytes_accessed=12 * 2**20, transcendentals=256),
        name="step",
    )(
        tokens, target, kv_weight[0], norm_gain,
        global_frag.reshape(256, 1024), momentum.reshape(256, 1024), local_frag.reshape(256, 1024),
    )
    return (wg[None], tg, gg.reshape(1, D), ng.reshape(2, 128, 1024), nm.reshape(2, 128, 1024))


def solution(mesh):
    placed = (
        P(("island", "fsdp"), None),
        P(("island", "fsdp"), None),
        P("island", "fsdp", None),
        P("island", None),
        P(None, "fsdp", None),
        P(None, "fsdp", None),
        P("island", None, "fsdp", None),
    )
    return jax.shard_map(
        on_device,
        mesh=mesh,
        in_specs=placed,
        out_specs=(
            P("island", "fsdp", None),
            P(("island", "fsdp"), None),
            P("island", None),
            P(None, "fsdp", None),
            P(None, "fsdp", None),
        ),
        check_vma=False,
    )
```

time: 369 us -> 109 us (0.30)
  waiting for transfers between devices: 184 us -> 0 us
  blocking collectives: 132 us -> 0 us
  Pallas kernels: 0 us -> 99.9 us
  matrix products: 22.3 us -> 0 us
  between operations: 15.5 us -> 0.65 us
  other arithmetic: 13 us -> 0 us
  local copies, waits for them, and re-layouts: 1.97 us -> 7.44 us
    psum x1 -> x0, blocking collectives: 132 us -> none  [on_device(): gain_grad = lax.psum(jnp.sum(back * scaled, axis=0), 'fsdp')]
    all_gather x1 -> x0, waiting for transfers between devices: 104 us -> none  [on_device(): full_weight = lax.all_gather(weight_shard, 'fsdp', axis=0, tiled=True)]
    pallas_call x0 -> x1, Pallas kernels: none -> 99.9 us  [on_device(): pl.pallas_call(kernel, out_shape=outs, in_specs=[anyspec] * 7, out_specs=...]
    reduce_scatter x1 -> x0, waiting for transfers between devices: 78.7 us -> none  [on_device(): lax.psum_scatter(loss_scale * product, 'fsdp', scatter_dimension=0, tiled...]
    dot_general x3 -> x0, matrix products: 22.3 us -> none  [the longest x1 8.35 us: on_device(): lax.dot_general(normed, error, (((0,), (0,)), ((), ())), preferred_elemen...]
    sub x2 -> x0, other arithmetic: 6.06 us -> none  [the longest x1 3.36 us: on_device(): new_global = global_frag - 0.7 * (outer_grad + 0.9 * new_momentum)]
    unnamed x12 -> x11, local copies, waits for them, and re-layouts: 1.97 us -> 7.44 us
    convert_element_type x1 -> x0, other arithmetic: 4.66 us -> none  [on_device(): token_grad = token_grad.astype(jnp.bfloat16)]
  transfers between devices with their start and end apart: 3 -> 0, of which waited for: 2 -> 0; matrix products, arithmetic and copies ran while one was open for 9% -> 0% of each run, Pallas kernels for 0% -> 0%
where the time goes in v1:
time: 109 us; the launch traced here: 108 us
  Pallas kernels  99.9 us (92%)
  local copies, waits for them, and re-layouts  7.44 us (7%)
    pallas_call x1, Pallas kernels, on_device(): pl.pallas_call(kernel, out_shape=outs, in_specs=[anyspec] * 7, out_specs=...  99.9 us
    unnamed x11, local copies, waits for them, and re-layouts  7.44 us

profile of v1, /device:TPU:2, one launch (start us, length us, event | category | flops | bytes accessed | tf_op | source)
XLA Modules:
  0.0 107.9 jit_solution(5327051929876220359)
XLA Ops:
  0.6 99.9 %step.1 = (bf16[128,1024]{1,0:T(8,128)(2,1)}, bf16[256,4096]{1,0:T(8,128)(2,1)}, f32[32,128]{1,0:T(8,128)}, f32[256,1024]{1,0:T(8,128)}, f32[256,1024]{1,0:T(8,128)}) custom-call(bf16[256,4096]{1,0:T(8,128)(2,1)} %tok_h.1, bf16[256,1024]{1,0:T(8,128)(2,1)} %tgt_h.1, bf16[128,1024]{1,0:T(8,128)(2,1)} %bitcast.15, f32[1,4096]{1,0:T(1,128)} %gain_h.1, ...), custom_call_target="tpu_custom_call" | custom-call | flops 6442450944 | bytes 12582912 | tf_op jit(solution)/shard_map/step/pallas_call | solution.py:351
  100.5 1.7 %copy.17 = bf16[1,128,1024]{2,1,0:T(8,128)(2,1)} copy(bf16[1,128,1024]{2,1,0:T(8,128)(2,1)} %bitcast.10) | data formatting | bytes 524288
  102.2 0.0 copy-start.2
  102.2 0.0 copy-start.1
  102.2 3.2 %copy.18 = bf16[256,4096]{1,0:T(8,128)(2,1)} copy(bf16[256,4096]{1,0:T(8,128)(2,1)} %get-tuple-element.21) | data formatting | bytes 4194304
  105.4 0.0 copy-done.2
  105.4 0.0 copy-start
  105.4 0.6 copy.19
  106.0 0.0 copy-done.1
  106.0 1.0 copy.20
  107.0 0.0 copy-done
  107.0 1.0 copy.21
Async XLA Ops:
  102.2 3.2 %copy-start.2 = (f32[32,128]{1,0:T(8,128)S(1)}, f32[32,128]{1,0:T(8,128)}, u32[]{:S(2)}) copy-start(f32[32,128]{1,0:T(8,128)} %get-tuple-element.12) | copy-start | bytes 49156
  102.2 3.8 %copy-start.1 = (f32[256,1024]{1,0:T(8,128)S(1)}, f32[256,1024]{1,0:T(8,128)}, u32[]{:S(2)}) copy-start(f32[256,1024]{1,0:T(8,128)} %get-tuple-element.13) | copy-start | bytes 3145732
  105.4 1.6 %copy-start = (f32[256,1024]{1,0:T(8,128)S(1)}, f32[256,1024]{1,0:T(8,128)}, u32[]{:S(2)}) copy-start(f32[256,1024]{1,0:T(8,128)} %get-tuple-element.14) | copy-start | bytes 3145732

commit v2 on v1

--- a/solution.py
+++ b/solution.py
@@ -89,7 +89,7 @@
     for q in range(NQ):
         loads_w[q].wait()
         push(own_half(q, yh), own_half(q, yh), y_sem.at[q], flip)
-        if q < 2:
+        if q < 3:
             ring_own(q, yh)
 
     def to_sib(q, zz):
@@ -239,101 +239,154 @@
 
     stores = []
 
-    def back_blocks(lo, hi):
+    def back_first(lo, hi):
         def one(kb, _):
             bc, bz = kb // 8, kb % 8
-            b = nt_dot(errb[0, 0], wb[0, bc, bz])
-            for q in range(1, NQ):
-                b += nt_dot(errb[0, q], wb[q, bc, bz])
+            b = nt_dot(errb[0, 0], wb[0, bc, bz]) + nt_dot(errb[0, 1], wb[1, bc, bz])
+            back[:, pl.ds(pl.multiple_of(kb * 256, 256), 256)] = b
+            return 0
+
+        lax.fori_loop(lo, hi, one, 0)
+
+    def back_rest(lo, hi):
+        def one(kb, _):
+            bc, bz = kb // 8, kb % 8
+            here = pl.ds(pl.multiple_of(kb * 256, 256), 256)
+            b = back[:, here] + nt_dot(errb[0, 2], wb[2, bc, bz]) + nt_dot(errb[0, 3], wb[3, bc, bz])
+            back[:, here] = b
             for by in range(2):
                 f = (bz * 2 + by) * 2 + bc
                 cols = pl.ds(pl.multiple_of(f * 128, 128), 128)
-                bb = b[:, by * 128:(by + 1) * 128]
-                sc = tok[:, cols].astype(F32) * inv_ref[...]
-                bs = bb * sc
+                bs = b[:, by * 128:(by + 1) * 128] * (tok[:, cols].astype(F32) * inv_ref[...])
                 go[pl.ds(f, 1), :] = jnp.sum(bs, axis=0, keepdims=True)
                 rowacc[...] += bs * gain[:, cols]
-                back[:, cols] = bb
             return 0
 
         lax.fori_loop(lo, hi, one, 0)
 
     def token_grad():
-        m = jnp.sum(rowacc[...], axis=1, keepdims=True) / D
-
-        def one(f, _):
+        m = jnp.broadcast_to(jnp.sum(rowacc[...], axis=1, keepdims=True) / D, (TOK, 128))
+
+        def one(i, _):
+            f = ((i // 2) % 8 * 2 + i % 2) * 2 + i // 16
             cols = pl.ds(pl.multiple_of(f * 128, 128), 128)
+            bb = back[:, pl.ds(pl.multiple_of(i * 128, 128), 128)]
             iv = inv_ref[...]
             sc = tok[:, cols].astype(F32) * iv
-            tgo[:, cols] = (iv * (back[:, cols] * gain[:, cols] - sc * m)).astype(BF16)
+            tgo[:, cols] = (iv * (bb * gain[:, cols] - sc * m)).astype(BF16)
             return 0
 
         lax.fori_loop(0, 32, one, 0)
         stores.append(pltpu.make_async_copy(tgo, tg_h, st.at[2]))
         stores[-1].start()
 
-    gather_step(0, 1)
-    drift_out()
-    gather_step(0, 2)
-    for q in (2, 3):
-        ring_own(q, yh)
-        ring_other(q)
-    for q in (2, 3):
-        to_sib(q, z)
-    gather_step(0, 3)
-    loads[2].wait()
-    gather_step(0, 4)
-    project(0)
-    gather_step(1, 1)
-    pass_error(0)
-    drift_sum()
-    gather_step(1, 2)
-    have_error(0)
-    for r in range(3):
-        arrived(ntr.at[r], nt_sem.at[r])
-    gather_step(1, 3)
-    outer_step()
-    gather_step(1, 4)
-    reduce_step(0, 0)
-    project(1)
-    reduce_step(0, 1)
-    pass_error(1)
-    rowacc[...] = jnp.zeros_like(rowacc)
-    reduce_step(0, 2)
-    have_error(1)
-    reduce_step(1, 0)
-    back_blocks(0, 8)
-    reduce_step(0, 3)
-    reduce_step(1, 1)
-    back_blocks(8, 16)
-    push(go, gc, g_sem.at[0], sib)
-    reduce_step(1, 2)
-    arrived(gc, g_sem.at[0])
-    g1[...] = go[...] + gc[...]
-    push(g1, gy, g_sem.at[1], flip)
-    reduce_last(0)
-    reduce_step(1, 3)
-    arrived(gy, g_sem.at[1])
-    g2[...] = g1[...] + gy[...]
-    for o in range(1, NZ):
-        push(g2, gz.at[z], gz_sem.at[z], at(mod8(z + o), yh, c))
-    gz[z] = g2[...]
-    token_grad()
-    reduce_last(1)
-    stores.append(pltpu.make_async_copy(wgo, wg_h, st.at[3]))
-    stores[-1].start()
-    for o in range(1, NZ):
-        zz = mod8(z + o)
-        arrived(gz.at[zz], gz_sem.at[zz])
-    total = gz[0]
-    for j in range(1, NZ):
-        total += gz[j]
-    gsum[...] = total
-    stores.append(pltpu.make_async_copy(gsum, gg_h, st.at[4]))
-    stores[-1].start()
+    def start_second():
+        ring_other(2)
+        ring_own(3, yh)
+        ring_other(3)
+        to_sib(2, z)
+        to_sib(3, z)
+
+    def transposes():
+        for r in range(3):
+            arrived(ntr.at[r], nt_sem.at[r])
+
+    def gain_core():
+        push(go, gc, g_sem.at[0], sib)
+
+    def gain_flip():
+        arrived(gc, g_sem.at[0])
+        g1[...] = go[...] + gc[...]
+        push(g1, gy, g_sem.at[1], flip)
+
+    def gain_ring():
+        arrived(gy, g_sem.at[1])
+        g2[...] = g1[...] + gy[...]
+        for o in range(1, NZ):
+            push(g2, gz.at[z], gz_sem.at[z], at(mod8(z + o), yh, c))
+        gz[z] = g2[...]
+
+    def gain_sum():
+        for o in range(1, NZ):
+            zz = mod8(z + o)
+            arrived(gz.at[zz], gz_sem.at[zz])
+        total = gz[0]
+        for j in range(1, NZ):
+            total += gz[j]
+        gsum[...] = total
+        stores.append(pltpu.make_async_copy(gsum, gg_h, st.at[4]))
+        stores[-1].start()
+
+    def weight_store():
+        stores.append(pltpu.make_async_copy(wgo, wg_h, st.at[3]))
+        stores[-1].start()
+
+    def zero_rows():
+        rowacc[...] = jnp.zeros_like(rowacc)
+
+    plan = (
+        (gather_step, 0, 1),
+        (drift_out,),
+        (gather_step, 0, 2),
+        (start_second,),
+        (gather_step, 0, 3),
+        (loads[2].wait,),
+        (gather_step, 0, 4),
+        (project, 0),
+        (gather_step, 1, 1),
+        (drift_sum,),
+        (back_first, 0, 8),
+        (gather_step, 1, 2),
+        (back_first, 8, 16),
+        (pass_error, 0),
+        (gather_step, 1, 3),
+        (have_error, 0),
+        (transposes,),
+        (reduce_step, 0, 0),
+        (outer_step,),
+        (zero_rows,),
+        (gather_step, 1, 4),
+        (project, 1),
+        (reduce_step, 0, 1),
+        (back_rest, 0, 4),
+        (pass_error, 1),
+        (reduce_step, 0, 2),
+        (have_error, 1),
+        (reduce_step, 1, 0),
+        (back_rest, 4, 10),
+        (reduce_step, 0, 3),
+        (reduce_step, 1, 1),
+        (back_rest, 10, 16),
+        (gain_core,),
+        (reduce_step, 1, 2),
+        (reduce_last, 0),
+        (gain_flip,),
+        (token_grad,),
+        (reduce_step, 1, 3),
+        (gain_ring,),
+        (reduce_last, 1),
+        (weight_store,),
+        (gain_sum,),
+    )
+    for stage, *args in plan:
+        stage(*args)
     for cp in sends:
         cp.wait_send()
     for cp in stores:
+        cp.wait()
+
+
+def hand_on(*refs):
+    n = len(refs) // 3
+    ins, outs, held, sems = refs[:n], refs[n:2 * n], refs[2 * n:3 * n], refs[3 * n]
+    first = [pltpu.make_async_copy(ins[i], held[i], sems.at[0, i]) for i in range(n)]
+    second = [pltpu.make_async_copy(held[i], outs[i], sems.at[1, i]) for i in range(n)]
+    for cp in first:
+        cp.start()
+    for a, b in zip(first, second):
+        a.wait()
+        b.start()
+    for cp in second:
         cp.wait()
 
 
@@ -404,6 +457,15 @@
         tokens, target, kv_weight[0], norm_gain,
         global_frag.reshape(256, 1024), momentum.reshape(256, 1024), local_frag.reshape(256, 1024),
     )
+    wg, tg, gg, ng, nm = pl.pallas_call(
+        hand_on,
+        out_shape=outs,
+        in_specs=[anyspec] * 5,
+        out_specs=[anyspec] * 5,
+        scratch_shapes=[vm(o.shape, o.dtype) for o in outs] + [sem((2, 5))],
+        compiler_params=pltpu.CompilerParams(vmem_limit_bytes=56 * 2**20),
+        name="hand_on",
+    )(wg, tg, gg, ng, nm)
     return (wg[None], tg, gg.reshape(1, D), ng.reshape(2, 128, 1024), nm.reshape(2, 128, 1024))
 
 

time: 109 us -> 102 us (0.936)
  local copies, waits for them, and re-layouts: 7.44 us -> 0 us
  Pallas kernels: 99.9 us -> 101 us
    unnamed x11 -> x0, local copies, waits for them, and re-layouts: 7.44 us -> none
    pallas_call x0 -> x1, Pallas kernels: none -> 3.79 us  [on_device(): pl.pallas_call(hand_on, out_shape=outs, in_specs=[anyspec] * 5, out_specs...]
    pallas_call x1, Pallas kernels: 99.9 us -> 97.3 us  [on_device(): pl.pallas_call(kernel, out_shape=outs, in_specs=[anyspec] * 7, out_specs=...]
where the time goes in v2:
time: 102 us
  Pallas kernels  101 us (99%)
    pallas_call x1, Pallas kernels, on_device(): pl.pallas_call(kernel, out_shape=outs, in_specs=[anyspec] * 7, out_specs=...  97.3 us
    pallas_call x1, Pallas kernels, on_device(): pl.pallas_call(hand_on, out_shape=outs, in_specs=[anyspec] * 5, out_specs...  3.79 us

profile of v2, /device:TPU:2, one launch (start us, length us, event | category | flops | bytes accessed | tf_op | source)
XLA Modules:
  0.0 101.7 jit_solution(8136939212347612939)
XLA Ops:
  0.6 97.3 %step.1 = (bf16[128,1024]{1,0:T(8,128)(2,1)}, bf16[256,4096]{1,0:T(8,128)(2,1)}, f32[32,128]{1,0:T(8,128)}, f32[256,1024]{1,0:T(8,128)}, f32[256,1024]{1,0:T(8,128)}) custom-call(bf16[256,4096]{1,0:T(8,128)(2,1)} %tok_h.1, bf16[256,1024]{1,0:T(8,128)(2,1)} %tgt_h.1, bf16[128,1024]{1,0:T(8,128)(2,1)} %bitcast.13, f32[1,4096]{1,0:T(1,128)} %gain_h.1, ...), custom_call_target="tpu_custom_call" | custom-call | flops 6442450944 | bytes 12582912 | tf_op jit(solution)/shard_map/step/pallas_call | solution.py:404
  97.9 3.8 %hand_on.1 = (bf16[128,1024]{1,0:T(8,128)(2,1)}, bf16[256,4096]{1,0:T(8,128)(2,1)}, f32[32,128]{1,0:T(8,128)}, f32[256,1024]{1,0:T(8,128)}, f32[256,1024]{1,0:T(8,128)}) custom-call(bf16[128,1024]{1,0:T(8,128)(2,1)} %get-tuple-element.15.refs_0_, bf16[256,4096]{1,0:T(8,128)(2,1)} %get-tuple-element.16.refs_1_, f32[32,128]{1,0:T(8,128)} %get-tuple-element.17.refs_2_, ...), custom_call_target="tpu_custom_call" | custom-call | tf_op jit(solution)/shard_map/hand_on/pallas_call | solution.py:460

commit v3 on v2

v3 whole, which is shorter than its diff:
```python
import math

import jax
import jax.numpy as jnp
from jax import lax
from jax.experimental import pallas as pl
from jax.experimental.pallas import tpu as pltpu
from jax.sharding import PartitionSpec as P

MESH = pl.DeviceIdType.MESH
BF16 = jnp.bfloat16
F32 = jnp.float32
GROUPS = ((0, 1), (2, 3))
WIDTH = (256, 256, 256, 256)
START = (0, 256, 512, 768)
NB = len(WIDTH)
SPLIT = (9, 9)
NZ = 8
NX = 4
TOK = 256
D = 4096
PLUS, MINUS = 0, 1
NSEND = 256


def hops(q, way):
    return 4 if (q % 2) == way else 3


def nt_dot(a, b):
    return lax.dot_general(a, b, (((1,), (1,)), ((), ())), preferred_element_type=F32)


def kernel(*refs):
    refs = list(refs)

    def take(n):
        out = refs[:n]
        del refs[:n]
        return out

    tok_h, tgt_h, w_h, gain_h, glob_h, mom_h, loc_h = take(7)
    wg_h, tg_h, gg_h, ng_h, nm_h = take(5)
    tok, tgt, gain, glob, mom, loc, normed, nto, ntr, back, tgo, wgo = take(12)
    dr, dp, dq, osb, go, gc, g1, gy, g2, gz, gsum, rowacc, inv_ref = take(13)
    wb, errb, rss, rsr = take(NB), take(NB), take(NB), take(NB)
    ld, st, send, ag_sem, y_sem, mix_sem, sib_sem, nt_sem, err_sem, rs_sem, d_sem, p_sem, o_sem, g_sem, gz_sem = take(15)

    isl = lax.axis_index("island")
    fs = lax.axis_index("fsdp")
    z = fs // 4
    yh = (fs // 2) % 2
    c = fs % 2
    yl = isl // NX
    x = isl % NX

    def at(zz, yy, cc):
        return (isl, (zz * 2 + yy) * 2 + cc)

    def mod8(v):
        return lax.rem(v + 8, 8)

    def along_x(o):
        return lax.rem(x + o, NX)

    ring = (at(mod8(z + 1), yh, c), at(mod8(z - 1), yh, c))
    sib = at(z, yh, 1 - c)
    flip = at(z, 1 - yh, c)
    diag = at(z, 1 - yh, 1 - c)
    low = ((1 - yl) * NX + x, fs)

    sends = []
    stores = []

    def push(src, dst, sem, dev):
        cp = pltpu.make_async_remote_copy(
            src_ref=src, dst_ref=dst, send_sem=send.at[len(sends)], recv_sem=sem,
            device_id=dev, device_id_type=MESH)
        cp.start()
        sends.append(cp)

    def arrived(ref, sem):
        pltpu.make_async_copy(ref, ref, sem).wait()

    def store(src, dst):
        cp = pltpu.make_async_copy(src, dst, st.at[len(stores)])
        cp.start()
        stores.append(cp)

    loads_w = [pltpu.make_async_copy(
        w_h.at[:, pl.ds(START[q], WIDTH[q])], wb[q].at[c, z, pl.ds(yh * 128, 128)], ld.at[q]) for q in range(NB)]
    for cp in loads_w:
        cp.start()
    loads = [pltpu.make_async_copy(s, d, ld.at[NB + i]) for i, (s, d) in enumerate(
        ((tok_h, tok), (gain_h, gain), (tgt_h, tgt), (glob_h, glob), (loc_h, loc), (mom_h, mom)))]
    for cp in loads:
        cp.start()

    bar = pltpu.get_barrier_semaphore()
    partners = [at(mod8(z + o), yh, c) for o in range(1, NZ)] + [sib, flip, diag, low]
    partners += [(yl * NX + along_x(o), fs) for o in range(1, NX)]
    for dev in partners:
        pl.semaphore_signal(bar, inc=1, device_id=dev, device_id_type=MESH)
    pl.semaphore_wait(bar, len(partners))

    def piece(q, zz):
        return wb[q].at[c, zz]

    def half(q, zz, yy):
        return wb[q].at[c, zz, pl.ds(yy * 128, 128)]

    def ring_own(q, yy):
        for way in (PLUS, MINUS):
            push(half(q, z, yy), half(q, z, yy), ag_sem.at[q, way, 0], ring[way])

    def to_sib(q, zz):
        push(piece(q, zz), piece(q, zz), sib_sem.at[q], sib)

    def ring_other(q):
        arrived(half(q, z, 1 - yh), y_sem.at[q])
        ring_own(q, 1 - yh)

    for q in range(NB):
        loads_w[q].wait()
        push(half(q, z, yh), half(q, z, yh), y_sem.at[q], flip)
        if q < 2:
            ring_own(q, yh)

    loads[0].wait()

    def squares(i, acc):
        t = tok[:, pl.ds(pl.multiple_of(i * 128, 128), 128)].astype(F32)
        return acc + t * t

    acc = lax.fori_loop(0, 32, squares, jnp.zeros((TOK, 128), F32), unroll=4)
    inv_ref[...] = jnp.broadcast_to(
        lax.rsqrt(jnp.sum(acc, axis=1, keepdims=True) / D + 1e-05), (TOK, 128))

    for q in (0, 1):
        ring_other(q)
    for q in (2, 3):
        ring_own(q, yh)
    for q in (0, 1):
        to_sib(q, z)

    loads[1].wait()

    def norm_block(i, _):
        bc, bz, by = i // 16, (i // 2) % 8, i % 2
        f = (bz * 2 + by) * 2 + bc
        cols = pl.ds(pl.multiple_of(f * 128, 128), 128)
        n = (tok[:, cols].astype(F32) * inv_ref[...] * gain[:, cols]).astype(BF16)
        normed[:, pl.ds(pl.multiple_of(i * 128, 128), 128)] = n
        nto[by, bc, bz] = n.T
        return 0

    lax.fori_loop(0, 32, norm_block, 0, unroll=2)
    push(nto.at[yh, 1 - c], ntr.at[0], nt_sem.at[0], sib)

    def send_normed(lo, hi):
        for zz in range(lo, hi):
            push(nto.at[1 - yh, c, zz], ntr.at[1, zz], nt_sem.at[1], flip)
            push(nto.at[1 - yh, 1 - c, zz], ntr.at[2, zz], nt_sem.at[2], diag)

    def have_normed():
        for r in range(3):
            arrived(ntr.at[r], nt_sem.at[r])

    def ring_group(g):
        for q in GROUPS[g]:
            if g > 1:
                ring_own(q, yh)
            ring_other(q)
        for q in GROUPS[g]:
            to_sib(q, z)

    def gather_step(g, s):
        for q in GROUPS[g]:
            for way in (PLUS, MINUS):
                k = hops(q, way)
                if s > k:
                    continue
                zz = mod8(z - s) if way == PLUS else mod8(z + s)
                if s < SPLIT[g]:
                    arrived(piece(q, zz), ag_sem.at[q, way, s - 1])
                else:
                    arrived(half(q, zz, yh), ag_sem.at[q, way, s - 1])
                if s < k:
                    block = piece(q, zz) if s + 1 < SPLIT[g] else half(q, zz, yh)
                    push(block, block, ag_sem.at[q, way, s], ring[way])
                if s < SPLIT[g]:
                    to_sib(q, zz)
                else:
                    push(half(q, zz, yh), half(q, zz, yh), mix_sem.at[q, way, s - 3], flip)

    def mix(g):
        for s in range(SPLIT[g], 5):
            for q in GROUPS[g]:
                for way in (PLUS, MINUS):
                    if s <= hops(q, way):
                        zz = mod8(z - s) if way == PLUS else mod8(z + s)
                        arrived(half(q, zz, 1 - yh), mix_sem.at[q, way, s - 3])
                        to_sib(q, zz)

    def project(g):
        for q in GROUPS[g]:
            w = WIDTH[q]
            arrived(wb[q].at[1 - c], sib_sem.at[q])
            p = jnp.dot(normed[...], wb[q][...].reshape(D, w), preferred_element_type=F32)
            errb[q][0] = (p - tgt[:, START[q]:START[q] + w].astype(F32)).astype(BF16)
            push(errb[q].at[0], errb[q].at[2], err_sem.at[1, q], flip)
            push(errb[q].at[0], errb[q].at[1], err_sem.at[0, q], sib)

    def pass_error(g):
        for q in GROUPS[g]:
            arrived(errb[q].at[2], err_sem.at[1, q])
            push(errb[q].at[2], errb[q].at[3], err_sem.at[2, q], sib)

    def have_error(g):
        for q in GROUPS[g]:
            arrived(errb[q].at[1], err_sem.at[0, q])
            arrived(errb[q].at[3], err_sem.at[2, q])

    def term(q, zz):
        p = jnp.dot(nto[yh, c, zz], errb[q][0], preferred_element_type=F32)
        for r in range(3):
            p += jnp.dot(ntr[r, zz], errb[q][r + 1], preferred_element_type=F32)
        return p

    def reduce_step(g, s):
        for q in GROUPS[g]:
            for way in (PLUS, MINUS):
                k = hops(q, way)
                if s >= k:
                    continue
                p = term(q, mod8(z + (k - s)) if way == PLUS else mod8(z - (k - s)))
                if s > 0:
                    arrived(rsr[q].at[way, s - 1], rs_sem.at[q, way, s - 1])
                    p += rsr[q][way, s - 1].astype(F32)
                rss[q][way, s] = p.astype(BF16)
                push(rss[q].at[way, s], rsr[q].at[way, s], rs_sem.at[q, way, s], ring[way])

    loss_scale = 1.0 / math.sqrt(TOK * 32)

    def reduce_last(g):
        for q in GROUPS[g]:
            p = term(q, z)
            for way in (PLUS, MINUS):
                s = hops(q, way) - 1
                arrived(rsr[q].at[way, s], rs_sem.at[q, way, s])
                p += rsr[q][way, s].astype(F32)
            cols = slice(START[q], START[q] + WIDTH[q])
            wgo[:, cols] = (p * loss_scale).astype(BF16)
        first = START[GROUPS[g][0]]
        cols = pl.ds(first, 2 * WIDTH[GROUPS[g][0]])
        store(wgo.at[:, cols], wg_h.at[:, cols])

    def x_rows(j):
        return pl.ds(pl.multiple_of(j * 64, 64), 64)

    def drift_out():
        loads[3].wait()
        loads[4].wait()

        def one(j, _):
            loc[x_rows(j), :] = glob[x_rows(j), :] - loc[x_rows(j), :]
            return 0

        lax.fori_loop(0, NX, one, 0)
        for o in range(1, NX):
            j = along_x(o)
            push(loc.at[x_rows(j)], dr.at[x], d_sem.at[x], (yl * NX + j, fs))
        dr[x] = loc[x_rows(x), :]

    def drift_pair():
        for o in range(1, NX):
            arrived(dr.at[along_x(o)], d_sem.at[along_x(o)])
        dp[...] = (dr[0] + dr[1]) + (dr[2] + dr[3])
        push(dp, dq, p_sem.at[0], low)

    def drift_back():
        arrived(dq, p_sem.at[0])
        osb[x] = (dp[...] + dq[...]) / 8
        for o in range(1, NX):
            push(osb.at[x], osb.at[x], o_sem.at[x], (yl * NX + along_x(o), fs))

    def outer_step():
        loads[5].wait()
        for o in range(1, NX):
            arrived(osb.at[along_x(o)], o_sem.at[along_x(o)])

        def one(j, _):
            rows = pl.ds(pl.multiple_of(j * 64, 64), 64)
            outer = osb[j]
            nm = 0.9 * mom[rows, :] + outer
            mom[rows, :] = nm
            glob[rows, :] = glob[rows, :] - 0.7 * (outer + 0.9 * nm)
            return 0

        lax.fori_loop(0, NX, one, 0)
        store(mom, nm_h)
        store(glob, ng_h)

    def back_part(g, lo, hi):
        def one(kb, _):
            bc, bz = kb // 8, kb % 8
            here = pl.ds(pl.multiple_of(kb * 256, 256), 256)
            b = nt_dot(errb[GROUPS[g][0]][0], wb[GROUPS[g][0]][bc, bz])
            b += nt_dot(errb[GROUPS[g][1]][0], wb[GROUPS[g][1]][bc, bz])
            back[:, here] = b if g == 0 else back[:, here] + b
            return 0

        lax.fori_loop(lo, hi, one, 0)

    def back_rest(lo, hi):
        def one(kb, _):
            bc, bz = kb // 8, kb % 8
            here = pl.ds(pl.multiple_of(kb * 256, 256), 256)
            b = back[:, here]
            for q in GROUPS[1]:
                b += nt_dot(errb[q][0], wb[q][bc, bz])
            back[:, here] = b
            for by in range(2):
                f = (bz * 2 + by) * 2 + bc
                cols = pl.ds(pl.multiple_of(f * 128, 128), 128)
                bs = b[:, by * 128:(by + 1) * 128] * (tok[:, cols].astype(F32) * inv_ref[...])
                go[pl.ds(f, 1), :] = jnp.sum(bs, axis=0, keepdims=True)
                rowacc[...] += bs * gain[:, cols]
            return 0

        lax.fori_loop(lo, hi, one, 0)

    def token_grad():
        m = jnp.broadcast_to(jnp.sum(rowacc[...], axis=1, keepdims=True) / D, (TOK, 128))

        def one(i, _):
            f = ((i // 2) % 8 * 2 + i % 2) * 2 + i // 16
            cols = pl.ds(pl.multiple_of(f * 128, 128), 128)
            bb = back[:, pl.ds(pl.multiple_of(i * 128, 128), 128)]
            iv = inv_ref[...]
            sc = tok[:, cols].astype(F32) * iv
            tgo[:, cols] = (iv * (bb * gain[:, cols] - sc * m)).astype(BF16)
            return 0

        lax.fori_loop(0, 32, one, 0)
        store(tgo, tg_h)

    def gain_core():
        push(go, gc, g_sem.at[0], sib)

    def gain_flip():
        arrived(gc, g_sem.at[0])
        g1[...] = go[...] + gc[...]
        push(g1, gy, g_sem.at[1], flip)

    def gain_ring():
        arrived(gy, g_sem.at[1])
        g2[...] = g1[...] + gy[...]
        for o in range(1, NZ):
            push(g2, gz.at[z], gz_sem.at[z], at(mod8(z + o), yh, c))
        gz[z] = g2[...]

    def gain_sum():
        for o in range(1, NZ):
            zz = mod8(z + o)
            arrived(gz.at[zz], gz_sem.at[zz])
        total = gz[0]
        for j in range(1, NZ):
            total += gz[j]
        gsum[...] = total
        store(gsum, gg_h)

    done = [0, 0]

    def settle():
        for cp in sends[done[0]:done[1]]:
            cp.wait_send()
        done[:] = [done[1], len(sends)]

    def zero_rows():
        rowacc[...] = jnp.zeros_like(rowacc)

    plan = (
        (gather_step, 0, 1),
        (drift_out,),
        (send_normed, 0, 8),
        (gather_step, 0, 2),
        (ring_group, 1),
        (gather_step, 0, 3),
        (settle,),
        (loads[2].wait,),
        (gather_step, 1, 1),
        (gather_step, 0, 4),
        (project, 0),
        (zero_rows,),
        (gather_step, 1, 2),
        (drift_pair,),
        (back_part, 0, 0, 16),
        (settle,),
        (gather_step, 1, 3),
        (pass_error, 0),
        (have_error, 0),
        (have_normed,),
        (reduce_step, 0, 0),
        (settle,),
        (gather_step, 1, 4),
        (project, 1),
        (drift_back,),
        (reduce_step, 0, 1),
        (pass_error, 1),
        (back_rest, 0, 3),
        (reduce_step, 0, 2),
        (have_error, 1),
        (reduce_step, 1, 0),
        (settle,),
        (back_rest, 3, 8),
        (reduce_step, 0, 3),
        (reduce_step, 1, 1),
        (back_rest, 8, 16),
        (gain_core,),
        (reduce_step, 1, 2),
        (reduce_last, 0),
        (gain_flip,),
        (settle,),
        (token_grad,),
        (reduce_step, 1, 3),
        (outer_step,),
        (gain_ring,),
        (settle,),
        (reduce_last, 1),
        (gain_sum,),
    )
    for stage, *args in plan:
        stage(*args)
    for cp in sends[done[0]:]:
        cp.wait_send()
    for cp in stores:
        cp.wait()


def hand_on(*refs):
    n = len(refs) // 3
    ins, outs, held, sems = refs[:n], refs[n:2 * n], refs[2 * n:3 * n], refs[3 * n]
    first = [pltpu.make_async_copy(ins[i], held[i], sems.at[0, i]) for i in range(n)]
    second = [pltpu.make_async_copy(held[i], outs[i], sems.at[1, i]) for i in range(n)]
    for cp in first:
        cp.start()
    for a, b in zip(first, second):
        a.wait()
        b.start()
    for cp in second:
        cp.wait()


def on_device(tokens, target, kv_weight, norm_gain, global_frag, momentum, local_frag):
    sem = pltpu.SemaphoreType.DMA
    vm = pltpu.VMEM
    anyspec = pl.BlockSpec(memory_space=pl.ANY)
    outs = (
        jax.ShapeDtypeStruct((128, 1024), BF16),
        jax.ShapeDtypeStruct((TOK, D), BF16),
        jax.ShapeDtypeStruct((32, 128), F32),
        jax.ShapeDtypeStruct((256, 1024), F32),
        jax.ShapeDtypeStruct((256, 1024), F32),
    )
    wg, tg, gg, ng, nm = pl.pallas_call(
        kernel,
        out_shape=outs,
        in_specs=[anyspec] * 7,
        out_specs=[anyspec] * 5,
        scratch_shapes=[
            vm((TOK, D), BF16),
            vm((TOK, 1024), BF16),
            vm((1, D), F32),
            vm((256, 1024), F32),
            vm((256, 1024), F32),
            vm((256, 1024), F32),
            vm((TOK, D), BF16),
            vm((2, 2, NZ, 128, TOK), BF16),
            vm((3, NZ, 128, TOK), BF16),
            vm((TOK, D), F32),
            vm((TOK, D), BF16),
            vm((128, 1024), BF16),
            vm((NX, 64, 1024), F32),
            vm((64, 1024), F32),
            vm((64, 1024), F32),
            vm((NX, 64, 1024), F32),
            vm((32, 128), F32),
            vm((32, 128), F32),
            vm((32, 128), F32),
            vm((32, 128), F32),
            vm((32, 128), F32),
            vm((NZ, 32, 128), F32),
            vm((32, 128), F32),
            vm((TOK, 128), F32),
            vm((TOK, 128), F32),
        ]
        + [vm((2, NZ, 256, w), BF16) for w in WIDTH]
        + [vm((4, TOK, w), BF16) for w in WIDTH]
        + [vm((2, 4, 128, w), BF16) for w in WIDTH]
        + [vm((2, 4, 128, w), BF16) for w in WIDTH]
        + [
            sem((NB + 6,)),
            sem((8,)),
            sem((NSEND,)),
            sem((NB, 2, 4)),
            sem((NB,)),
            sem((NB, 2, 2)),
            sem((NB,)),
            sem((3,)),
            sem((3, NB)),
            sem((NB, 2, 4)),
            sem((NX,)),
            sem((1,)),
            sem((NX,)),
            sem((2,)),
            sem((NZ,)),
        ],
        compiler_params=pltpu.CompilerParams(
            collective_id=0, has_side_effects=True, vmem_limit_bytes=60 * 2**20),
        cost_estimate=pl.CostEstimate(flops=6 * 2**30, bytes_accessed=12 * 2**20, transcendentals=256),
        name="step",
    )(
        tokens, target, kv_weight[0], norm_gain,
        global_frag.reshape(256, 1024), momentum.reshape(256, 1024), local_frag.reshape(256, 1024),
    )
    wg, tg, gg, ng, nm = pl.pallas_call(
        hand_on,
        out_shape=outs,
        in_specs=[anyspec] * 5,
        out_specs=[anyspec] * 5,
        scratch_shapes=[vm(o.shape, o.dtype) for o in outs] + [sem((2, 5))],
        compiler_params=pltpu.CompilerParams(vmem_limit_bytes=56 * 2**20),
        name="hand_on",
    )(wg, tg, gg, ng, nm)
    return (wg[None], tg, gg.reshape(1, D), ng.reshape(2, 128, 1024), nm.reshape(2, 128, 1024))


def solution(mesh):
    placed = (
        P(("island", "fsdp"), None),
        P(("island", "fsdp"), None),
        P("island", "fsdp", None),
        P("island", None),
        P(None, "fsdp", None),
        P(None, "fsdp", None),
        P("island", None, "fsdp", None),
    )
    return jax.shard_map(
        on_device,
        mesh=mesh,
        in_specs=placed,
        out_specs=(
            P("island", "fsdp", None),
            P(("island", "fsdp"), None),
            P("island", None),
            P(None, "fsdp", None),
            P(None, "fsdp", None),
        ),
        check_vma=False,
    )
```

time: 102 us -> 96.3 us (0.944)
  Pallas kernels: 101 us -> 95.6 us
    pallas_call x1, Pallas kernels: 97.3 us -> 91.8 us  [on_device(): pl.pallas_call(kernel, out_shape=outs, in_specs=[anyspec] * 7, out_specs=...]
where the time goes in v3:
time: 96.3 us; the launch traced here: 96.2 us
  Pallas kernels  95.6 us (99%)
    pallas_call x1, Pallas kernels, on_device(): pl.pallas_call(kernel, out_shape=outs, in_specs=[anyspec] * 7, out_specs=...  91.8 us
    pallas_call x1, Pallas kernels, on_device(): pl.pallas_call(hand_on, out_shape=outs, in_specs=[anyspec] * 5, out_specs...  3.79 us

profile of v3, /device:TPU:2, one launch (start us, length us, event | category | flops | bytes accessed | tf_op | source)
XLA Modules:
  0.0 96.2 jit_solution(15299327648746256562)
XLA Ops:
  0.6 91.8 %step.1 = (bf16[128,1024]{1,0:T(8,128)(2,1)}, bf16[256,4096]{1,0:T(8,128)(2,1)}, f32[32,128]{1,0:T(8,128)}, f32[256,1024]{1,0:T(8,128)}, f32[256,1024]{1,0:T(8,128)}) custom-call(bf16[256,4096]{1,0:T(8,128)(2,1)} %refs_0_.1, bf16[256,1024]{1,0:T(8,128)(2,1)} %refs_1_.1, bf16[128,1024]{1,0:T(8,128)(2,1)} %bitcast.13, f32[1,4096]{1,0:T(1,128)} %refs_3_.1, ...), custom_call_target="tpu_custom_call" | custom-call | flops 6442450944 | bytes 12582912 | tf_op jit(solution)/shard_map/step/pallas_call | solution.py:466
  92.5 3.8 %hand_on.1 = (bf16[128,1024]{1,0:T(8,128)(2,1)}, bf16[256,4096]{1,0:T(8,128)(2,1)}, f32[32,128]{1,0:T(8,128)}, f32[256,1024]{1,0:T(8,128)}, f32[256,1024]{1,0:T(8,128)}) custom-call(bf16[128,1024]{1,0:T(8,128)(2,1)} %get-tuple-element.15.refs_0_, bf16[256,4096]{1,0:T(8,128)(2,1)} %get-tuple-element.16.refs_1_, f32[32,128]{1,0:T(8,128)} %get-tuple-element.17.refs_2_, ...), custom_call_target="tpu_custom_call" | custom-call | tf_op jit(solution)/shard_map/hand_on/pallas_call | solution.py:527

commit v4 on v3

--- a/solution.py
+++ b/solution.py
@@ -407,9 +407,9 @@
         (project, 1),
         (drift_back,),
         (reduce_step, 0, 1),
-        (pass_error, 1),
         (back_rest, 0, 3),
         (reduce_step, 0, 2),
+        (pass_error, 1),
         (have_error, 1),
         (reduce_step, 1, 0),
         (settle,),

time: 96.3 us -> 93.9 us (0.975)
  Pallas kernels: 95.6 us -> 93.2 us
    pallas_call x1, Pallas kernels: 91.8 us -> 89.4 us  [on_device(): pl.pallas_call(kernel, out_shape=outs, in_specs=[anyspec] * 7, out_specs=...]
where the time goes in v4:
time: 93.9 us; the launch traced here: 93.8 us
  Pallas kernels  93.2 us (99%)
    pallas_call x1, Pallas kernels, on_device(): pl.pallas_call(kernel, out_shape=outs, in_specs=[anyspec] * 7, out_specs=...  89.4 us
    pallas_call x1, Pallas kernels, on_device(): pl.pallas_call(hand_on, out_shape=outs, in_specs=[anyspec] * 5, out_specs...  3.79 us

profile of v4, /device:TPU:2, one launch (start us, length us, event | category | flops | bytes accessed | tf_op | source)
XLA Modules:
  0.0 93.8 jit_solution(11366654545384588275)
XLA Ops:
  0.6 89.4 %step.1 = (bf16[128,1024]{1,0:T(8,128)(2,1)}, bf16[256,4096]{1,0:T(8,128)(2,1)}, f32[32,128]{1,0:T(8,128)}, f32[256,1024]{1,0:T(8,128)}, f32[256,1024]{1,0:T(8,128)}) custom-call(bf16[256,4096]{1,0:T(8,128)(2,1)} %refs_0_.1, bf16[256,1024]{1,0:T(8,128)(2,1)} %refs_1_.1, bf16[128,1024]{1,0:T(8,128)(2,1)} %bitcast.13, f32[1,4096]{1,0:T(1,128)} %refs_3_.1, ...), custom_call_target="tpu_custom_call" | custom-call | flops 6442450944 | bytes 12582912 | tf_op jit(solution)/shard_map/step/pallas_call | solution.py:466
  90.0 3.8 %hand_on.1 = (bf16[128,1024]{1,0:T(8,128)(2,1)}, bf16[256,4096]{1,0:T(8,128)(2,1)}, f32[32,128]{1,0:T(8,128)}, f32[256,1024]{1,0:T(8,128)}, f32[256,1024]{1,0:T(8,128)}) custom-call(bf16[128,1024]{1,0:T(8,128)(2,1)} %get-tuple-element.15.refs_0_, bf16[256,4096]{1,0:T(8,128)(2,1)} %get-tuple-element.16.refs_1_, f32[32,128]{1,0:T(8,128)} %get-tuple-element.17.refs_2_, ...), custom_call_target="tpu_custom_call" | custom-call | tf_op jit(solution)/shard_map/hand_on/pallas_call | solution.py:527
